TPU v7x, 32 devices: a whole 2x2x4 slice. The times are simulated.
32 devices in a mesh: section: 1, expert: 32 (over z, y, x, core).
Axes of the slice: x: 2, y: 2, z: 4, core: 2. Of those that a mesh axis runs over, the one named last changes fastest.
Arguments:
- acts: bfloat16 [1, 2, 2048, 3584], P('section', None, 'expert'), may hold values from -6 to 6
- norm_gain: float32 [1, 3584], P('section'), may hold values from 0.1 to 1.9
- router: bfloat16 [1, 3584, 8], P('section'), may hold values from -0.09375 to 0.09375
- routes: int32 [1, 2, 2, 2048, 1], P('section', None, None, 'expert'), may hold values from 0 to 7; in each aligned block of 64 rows (0 to 63, 64 to 127, ..., all dimensions but the last counted through in order) at most 16 rows name the same one
- w_gate: bfloat16 [1, 32, 3584, 256], P('section', 'expert'), may hold values from -0.09375 to 0.09375
- w_up: bfloat16 [1, 32, 3584, 256], P('section', 'expert'), may hold values from -0.09375 to 0.09375
- w_down: bfloat16 [1, 32, 256, 3584], P('section', 'expert'), may hold values from -0.375 to 0.375
Outputs:
- finished: bfloat16 [1, 2, 2048, 3584], P('section', None, 'expert')
Inputs may be any that keep to these rules, and one draw needn't show every extreme that they name: `routes`: within each block of 64 tokens of one device, for each layer, round and micro-batch, no expert is named by more than 16 tokens, a bound that some block reaches.
All inputs are finite; a program needn't handle non-finite values.
Results may differ from a plain program's by a relative error of at most 0.0072.
Values may be sent and summed in bfloat16 or wider, within the bound.
A program may use at most 128 MiB of HBM per device.

v0:
```python
import jax
import jax.numpy as jnp
from jax import lax
from jax.sharding import PartitionSpec as P


def for_sending(shard):

    def short(part):
        return part.astype(jnp.bfloat16) if part.dtype == jnp.float32 else part

    return jax.tree.map(short, shard)


def passed_along(value, axis, steps):
    count = lax.axis_size(axis)
    pairs = [(source, (source + steps) % count) for source in range(count)]
    return lax.ppermute(value, axis, pairs)


def body(acts, norm_gain, router, routes, w_gate, w_up, w_down):
    devices = lax.axis_size("expert")
    experts_here = router.shape[2]
    group_size = devices // experts_here
    tok_local = acts.shape[2]
    width = acts.shape[3]
    capacity = 2 * tok_local // experts_here
    gain_row = norm_gain[0]
    router_mat = router[0]
    gate_mat = w_gate[0, 0]
    up_mat = w_up[0, 0]
    down_mat = w_down[0, 0]

    def expert_compute(rows_box):
        count = rows_box.shape[1]
        rows_in = rows_box.reshape(devices * count, width)
        gate_proj = jnp.dot(rows_in, gate_mat, preferred_element_type=jnp.float32)
        up_proj = jnp.dot(rows_in, up_mat, preferred_element_type=jnp.float32)
        hidden = (jax.nn.silu(gate_proj) * up_proj).astype(jnp.bfloat16)
        partial_out = jnp.dot(hidden, down_mat, preferred_element_type=jnp.float32).astype(
            jnp.bfloat16
        )
        return partial_out.reshape(devices, count, width)

    def expert_work(rows_box):
        return lax.all_to_all(
            expert_compute(rows_box), "expert", split_axis=0, concat_axis=0, tiled=True
        )

    def apply_layer(tokens_in, route_ids):
        x_float = tokens_in.astype(jnp.float32)
        mean_sq = jnp.mean(x_float * x_float, axis=1, keepdims=True)
        normed = (x_float * lax.rsqrt(mean_sq + 1e-06) * gain_row[None, :]).astype(jnp.bfloat16)
        scores = jnp.dot(normed, router_mat, preferred_element_type=jnp.float32)
        chosen = route_ids[:, 0]
        onehot = (chosen[:, None] == jnp.arange(experts_here, dtype=jnp.int32)[None, :]).astype(
            jnp.int32
        )
        gate_val = jax.nn.sigmoid(jnp.sum(scores * onehot.astype(jnp.float32), axis=1))
        slot_of = jnp.sum(jnp.cumsum(onehot, axis=0) * onehot, axis=1) - 1
        flat_slot = chosen * capacity + slot_of
        placing = (
            flat_slot[None, :] == jnp.arange(experts_here * capacity, dtype=jnp.int32)[:, None]
        ).astype(jnp.bfloat16)
        outbox = jnp.dot(placing, normed, preferred_element_type=jnp.float32).astype(jnp.bfloat16)
        outbox = outbox.reshape(experts_here, capacity, width)
        sendout = jnp.broadcast_to(outbox[None], (group_size, experts_here, capacity, width))
        sendout = sendout.reshape(devices, capacity, width)
        returned = expert_work(
            lax.all_to_all(sendout, "expert", split_axis=0, concat_axis=0, tiled=True)
        )
        combined = jnp.sum(
            returned.reshape(group_size, experts_here, capacity, width).astype(jnp.float32), axis=0
        )
        combined = combined.reshape(experts_here * capacity, width)
        picked = jnp.take(combined, flat_slot, axis=0)
        return (x_float + gate_val[:, None] * picked).astype(jnp.bfloat16)

    micro_count = acts.shape[1]
    carried = [acts[0, micro_idx] for micro_idx in range(micro_count)]
    for round_idx in range(routes.shape[1]):
        updated_all = [
            apply_layer(carried[micro_idx], routes[0, round_idx, micro_idx])
            for micro_idx in range(micro_count)
        ]
        carried = list(passed_along(for_sending(tuple(updated_all)), "section", 1))
    return jnp.stack(carried)[None]


def solution(mesh):
    in_specs = (
        P("section", None, "expert", None),
        P("section", None),
        P("section", None, None),
        P("section", None, None, "expert", None),
        P("section", "expert", None, None),
        P("section", "expert", None, None),
        P("section", "expert", None, None),
    )
    out_specs = P("section", None, "expert", None)
    return jax.shard_map(body, mesh=mesh, in_specs=in_specs, out_specs=out_specs, check_vma=False)
```

profile of v0, /device:TPU:11, one launch (start us, length us, event | category | flops | bytes accessed | tf_op | source)
XLA Modules:
  0.0 735.5 jit_solution(10950301516938729743)
XLA Ops:
  0.0 1.6 fusion.62
  1.6 0.7 slice_bitcast_fusion.2
  3.3 0.8 reduce
  4.1 0.7 compare_and_fusion.2
  4.9 1.5 convolution_convert_fusion.7
  6.3 2.3 broadcast_in_dim.28
  8.6 6.4 all-to-all-start
  15.0 1.4 convolution_convert_fusion.5
  16.4 78.7 %all-to-all-done = bf16[32,16,3584]{2,1,0:T(8,128)(2,1)} async-done(((bf16[32,16,3584]{2,1,0:T(8,128)(2,1)}), bf16[32,16,3584]{2,1,0:T(8,128)(2,1)}, u32[]{:S(2)}, u32[]{:S(2)}) %all-to-all-start) | async-done | bytes 3670048 | tf_op jit(solution)/shard_map/all_to_all | solution.py:70
  95.1 3.5 broadcast_in_dim.32
  98.6 6.7 all-to-all-start.4
  105.2 4.5 fusion.18
  109.8 8.5 %convolution_convert_fusion.3 = bf16[512,3584]{1,0:T(8,128)(2,1)} fusion(bf16[1,1,256,3584]{3,2,1,0:T(8,128)(2,1)S(1)} %copy-done, bf16[512,3584]{1,0:T(8,128)(2,1)} %bitcast.6, bf16[1,1,3584,256]{3,2,1,0:T(8,128)(2,1)} %param.14, f32[512,256]{1,0:T(8,128)} %fusion.18), kind=kOutput, calls=%fused_computation.11 | convolution fusion | flops 1881669632 | bytes 11534336 | tf_op jit(solution)/shard_map/dot_general | solution.py:40
  118.3 67.0 %all-to-all-done.4 = bf16[32,16,3584]{2,1,0:T(8,128)(2,1)} async-done(((bf16[32,16,3584]{2,1,0:T(8,128)(2,1)}), bf16[32,16,3584]{2,1,0:T(8,128)(2,1)}, u32[]{:S(2)}, u32[]{:S(2)}) %all-to-all-start.4) | async-done | bytes 3670048 | tf_op jit(solution)/shard_map/all_to_all | solution.py:70
  185.3 6.7 all-to-all-start.1
  192.0 4.5 fusion.14
  196.5 8.5 %convolution_convert_fusion.1 = bf16[512,3584]{1,0:T(8,128)(2,1)} fusion(bf16[1,1,256,3584]{3,2,1,0:T(8,128)(2,1)S(1)} %copy-done, bf16[512,3584]{1,0:T(8,128)(2,1)} %bitcast.26, bf16[1,1,3584,256]{3,2,1,0:T(8,128)(2,1)} %param.14, f32[512,256]{1,0:T(8,128)} %fusion.14), kind=kOutput, calls=%fused_computation.9 | convolution fusion | flops 1881669632 | bytes 11534336 | tf_op jit(solution)/shard_map/dot_general | solution.py:40
  205.0 67.0 %all-to-all-done.1 = bf16[32,16,3584]{2,1,0:T(8,128)(2,1)} async-done(((bf16[32,16,3584]{2,1,0:T(8,128)(2,1)}), bf16[32,16,3584]{2,1,0:T(8,128)(2,1)}, u32[]{:S(2)}, u32[]{:S(2)}) %all-to-all-start.1) | async-done | bytes 3670048 | tf_op jit(solution)/shard_map/all_to_all | solution.py:46
  272.1 6.7 all-to-all-start.5
  279.5 4.1 convert_reduce_fusion.3
  283.5 75.3 %all-to-all-done.5 = bf16[32,16,3584]{2,1,0:T(8,128)(2,1)} async-done(((bf16[32,16,3584]{2,1,0:T(8,128)(2,1)}), bf16[32,16,3584]{2,1,0:T(8,128)(2,1)}, u32[]{:S(2)}, u32[]{:S(2)}) %all-to-all-start.5) | async-done | bytes 3670048 | tf_op jit(solution)/shard_map/all_to_all | solution.py:46
  358.8 4.0 convert_reduce_fusion.1
  362.8 3.7 gather_fusion
  366.5 3.7 gather_fusion.2
  370.1 1.8 fusion.65
  372.2 0.5 convolution_convert_fusion.4
  372.7 2.3 broadcast_in_dim.34
  374.9 6.7 all-to-all-start.6
  381.9 1.4 convolution_convert_fusion.6
  383.3 78.4 %all-to-all-done.6 = bf16[32,16,3584]{2,1,0:T(8,128)(2,1)} async-done(((bf16[32,16,3584]{2,1,0:T(8,128)(2,1)}), bf16[32,16,3584]{2,1,0:T(8,128)(2,1)}, u32[]{:S(2)}, u32[]{:S(2)}) %all-to-all-start.6) | async-done | bytes 3670048 | tf_op jit(solution)/shard_map/all_to_all | solution.py:70
  461.7 3.5 broadcast_in_dim.30
  465.2 6.7 all-to-all-start.2
  471.8 4.5 fusion.12
  476.4 8.5 %convolution_convert_fusion = bf16[512,3584]{1,0:T(8,128)(2,1)} fusion(bf16[1,1,256,3584]{3,2,1,0:T(8,128)(2,1)S(1)} %copy-done, bf16[512,3584]{1,0:T(8,128)(2,1)} %bitcast.33, bf16[1,1,3584,256]{3,2,1,0:T(8,128)(2,1)} %param.14, f32[512,256]{1,0:T(8,128)} %fusion.12), kind=kOutput, calls=%fused_computation.8 | convolution fusion | flops 1881669632 | bytes 11534336 | tf_op jit(solution)/shard_map/dot_general | solution.py:40
  484.9 67.0 %all-to-all-done.2 = bf16[32,16,3584]{2,1,0:T(8,128)(2,1)} async-done(((bf16[32,16,3584]{2,1,0:T(8,128)(2,1)}), bf16[32,16,3584]{2,1,0:T(8,128)(2,1)}, u32[]{:S(2)}, u32[]{:S(2)}) %all-to-all-start.2) | async-done | bytes 3670048 | tf_op jit(solution)/shard_map/all_to_all | solution.py:70
  551.9 6.7 all-to-all-start.7
  558.6 4.5 fusion.16
  563.1 8.4 %convolution_convert_fusion.2 = bf16[512,3584]{1,0:T(8,128)(2,1)} fusion(bf16[1,1,256,3584]{3,2,1,0:T(8,128)(2,1)S(1)} %copy-done, bf16[512,3584]{1,0:T(8,128)(2,1)} %bitcast.16, bf16[1,1,3584,256]{3,2,1,0:T(8,128)(2,1)} %param.14, f32[512,256]{1,0:T(8,128)} %fusion.16), kind=kOutput, calls=%fused_computation.10 | convolution fusion | flops 1881669632 | bytes 11534336 | tf_op jit(solution)/shard_map/dot_general | solution.py:40
  571.5 67.1 %all-to-all-done.7 = bf16[32,16,3584]{2,1,0:T(8,128)(2,1)} async-done(((bf16[32,16,3584]{2,1,0:T(8,128)(2,1)}), bf16[32,16,3584]{2,1,0:T(8,128)(2,1)}, u32[]{:S(2)}, u32[]{:S(2)}) %all-to-all-start.7) | async-done | bytes 3670048 | tf_op jit(solution)/shard_map/all_to_all | solution.py:46
  638.7 6.7 all-to-all-start.3
  646.0 4.0 convert_reduce_fusion
  650.0 3.7 gather_fusion.3
  653.7 1.4 fusion.81
  655.1 70.3 %all-to-all-done.3 = bf16[32,16,3584]{2,1,0:T(8,128)(2,1)} async-done(((bf16[32,16,3584]{2,1,0:T(8,128)(2,1)}), bf16[32,16,3584]{2,1,0:T(8,128)(2,1)}, u32[]{:S(2)}, u32[]{:S(2)}) %all-to-all-start.3) | async-done | bytes 3670048 | tf_op jit(solution)/shard_map/all_to_all | solution.py:46
  725.4 4.0 convert_reduce_fusion.2
  729.4 3.7 gather_fusion.1
  733.1 1.4 fusion.77
  734.5 1.0 maximum_bitcast_fusion
  (53 shorter events, 3.0 us)
Async XLA Ops:
  0.0 109.8 %copy-start = (bf16[1,1,256,3584]{3,2,1,0:T(8,128)(2,1)S(1)}, bf16[1,1,256,3584]{3,2,1,0:T(8,128)(2,1)}, u32[]{:S(2)}) copy-start(bf16[1,1,256,3584]{3,2,1,0:T(8,128)(2,1)} %param.15) | copy-start | bytes 5505028
  8.6 6.4 copy-start.1
  8.6 86.5 %all-to-all-start = ((bf16[32,16,3584]{2,1,0:T(8,128)(2,1)}), bf16[32,16,3584]{2,1,0:T(8,128)(2,1)}, u32[]{:S(2)}, u32[]{:S(2)}) async-start(bf16[32,16,3584]{2,1,0:T(8,128)(2,1)} %bitcast.167), calls=%async_computation | async-start | bytes 7340032 | tf_op jit(solution)/shard_map/all_to_all | solution.py:70
  98.6 86.7 %all-to-all-start.4 = ((bf16[32,16,3584]{2,1,0:T(8,128)(2,1)}), bf16[32,16,3584]{2,1,0:T(8,128)(2,1)}, u32[]{:S(2)}, u32[]{:S(2)}) async-start(bf16[32,16,3584]{2,1,0:T(8,128)(2,1)} %bitcast.165), calls=%async_computation.4 | async-start | bytes 7340032 | tf_op jit(solution)/shard_map/all_to_all | solution.py:70
  185.3 86.7 %all-to-all-start.1 = ((bf16[32,16,3584]{2,1,0:T(8,128)(2,1)}), bf16[32,16,3584]{2,1,0:T(8,128)(2,1)}, u32[]{:S(2)}, u32[]{:S(2)}) async-start(bf16[32,16,3584]{2,1,0:T(8,128)(2,1)} %bitcast.170), calls=%async_computation.1 | async-start | bytes 7340032 | tf_op jit(solution)/shard_map/all_to_all | solution.py:46
  272.1 6.7 copy-start.2
  272.1 86.7 %all-to-all-start.5 = ((bf16[32,16,3584]{2,1,0:T(8,128)(2,1)}), bf16[32,16,3584]{2,1,0:T(8,128)(2,1)}, u32[]{:S(2)}, u32[]{:S(2)}) async-start(bf16[32,16,3584]{2,1,0:T(8,128)(2,1)} %bitcast.169), calls=%async_computation.5 | async-start | bytes 7340032 | tf_op jit(solution)/shard_map/all_to_all | solution.py:46
  374.9 86.7 %all-to-all-start.6 = ((bf16[32,16,3584]{2,1,0:T(8,128)(2,1)}), bf16[32,16,3584]{2,1,0:T(8,128)(2,1)}, u32[]{:S(2)}, u32[]{:S(2)}) async-start(bf16[32,16,3584]{2,1,0:T(8,128)(2,1)} %bitcast.164), calls=%async_computation.6 | async-start | bytes 7340032 | tf_op jit(solution)/shard_map/all_to_all | solution.py:70
  465.2 86.7 %all-to-all-start.2 = ((bf16[32,16,3584]{2,1,0:T(8,128)(2,1)}), bf16[32,16,3584]{2,1,0:T(8,128)(2,1)}, u32[]{:S(2)}, u32[]{:S(2)}) async-start(bf16[32,16,3584]{2,1,0:T(8,128)(2,1)} %bitcast.166), calls=%async_computation.2 | async-start | bytes 7340032 | tf_op jit(solution)/shard_map/all_to_all | solution.py:70
  551.9 86.7 %all-to-all-start.7 = ((bf16[32,16,3584]{2,1,0:T(8,128)(2,1)}), bf16[32,16,3584]{2,1,0:T(8,128)(2,1)}, u32[]{:S(2)}, u32[]{:S(2)}) async-start(bf16[32,16,3584]{2,1,0:T(8,128)(2,1)} %bitcast.171), calls=%async_computation.7 | async-start | bytes 7340032 | tf_op jit(solution)/shard_map/all_to_all | solution.py:46
  638.7 86.7 %all-to-all-start.3 = ((bf16[32,16,3584]{2,1,0:T(8,128)(2,1)}), bf16[32,16,3584]{2,1,0:T(8,128)(2,1)}, u32[]{:S(2)}, u32[]{:S(2)}) async-start(bf16[32,16,3584]{2,1,0:T(8,128)(2,1)} %bitcast.168), calls=%async_computation.3 | async-start | bytes 7340032 | tf_op jit(solution)/shard_map/all_to_all | solution.py:46
  655.1 79.4 %collective-permute-start.3 = (bf16[64,3584]{1,0:T(8,128)(2,1)S(1)}, bf16[64,3584]{1,0:T(8,128)(2,1)S(1)}, u32[]{:S(2)}, u32[]{:S(2)}) collective-permute-start(bf16[64,3584]{1,0:T(8,128)(2,1)S(1)} %fusion.81), channel_id=1, source_target_pairs={{0,0},{1,1},{2,2},{3,3},{4,4},{5,5},{6,6},{7,7},{8,8},{9,9},{10,10... | collective-permute-start | bytes 1376264 | tf_op jit(solution)/shard_map/ppermute | solution.py:18
  734.5 0.1 collective-permute-start.1
  (2 other events, 0.1 us)
where the time goes:
time: 740 us; the launch traced here: 736 us
  waiting for transfers between devices  571 us (77%)
  matrix products  58 us (8%)
  starting transfers between devices  53.1 us (7%)
  local copies, waits for them, and re-layouts  27.5 us (4%)
  other arithmetic  25.7 us (3%)
    all_to_all x4, waiting for transfers between devices, apply_layer(): lax.all_to_all(sendout, 'expert', split_axis=0, concat_axis=0, tiled=True)  291 us
    all_to_all x4, waiting for transfers between devices, expert_work(): lax.all_to_all(expert_compute(rows_box), 'expert', split_axis=0, concat_a...  280 us
    dot_general x4, matrix products, expert_compute(): jnp.dot(hidden, down_mat, preferred_element_type=jnp.float32)  34 us
    all_to_all x4, starting transfers between devices, expert_work(): lax.all_to_all(expert_compute(rows_box), 'expert', split_axis=0, concat_a...  26.6 us
    all_to_all x4, starting transfers between devices, apply_layer(): lax.all_to_all(sendout, 'expert', split_axis=0, concat_axis=0, tiled=True)  26.3 us
    dot_general x4, matrix products, expert_compute(): gate_proj = jnp.dot(rows_in, gate_mat, preferred_element_type=jnp.float32)  18.1 us
    reduce_sum x4, other arithmetic, apply_layer(): jnp.sum(returned.reshape(group_size, experts_here, capacity, width).astyp...  16.1 us
  transfers between devices with their start and end apart: 12, of which 8 were waited for; matrix products, arithmetic and copies ran while one was open for 11% of the time, Pallas kernels for 0%

commit v1 on v0

v1 whole, which is shorter than its diff:
```python
import functools

import jax
import jax.numpy as jnp
from jax import lax
from jax.experimental import pallas as pl
from jax.experimental.pallas import tpu as pltpu
from jax.sharding import PartitionSpec as P

MESH = pl.DeviceIdType.MESH


def flipped(value, flips, count):
    total, bit = 0, 1
    while bit < count:
        total = total + bit * (((value // bit) % 2 + (flips // bit) % 2) % 2)
        bit *= 2
    return total


def column_tile(width):
    for tile in (512, 256, 128):
        if width % tile == 0:
            return tile
    return width


def layers_kernel(
    rounds,
    micros,
    planes,
    experts,
    capacity,
    acts_ref,
    gain_ref,
    router_ref,
    route_rows_ref,
    route_cols_ref,
    gate_ref,
    up_ref,
    down_ref,
    out_ref,
    peer_routes,
    tokens,
    outbox,
    inbox,
    partial,
    returned,
    plane_send,
    plane_back,
    route_send_sem,
    route_recv_sem,
    token_send_sem,
    token_recv_sem,
    out_send_sem,
    in_recv_sem,
    part_send_sem,
    ret_recv_sem,
    back_send_sem,
    back_recv_sem,
):
    me = lax.axis_index("expert")
    plane, place = me // experts, me % experts
    tok, width = acts_ref.shape[1], acts_ref.shape[2]
    tile = column_tile(width)
    tiles = width // tile
    slots = experts * capacity

    def cols(c):
        return pl.ds(pl.multiple_of(c * tile, tile), tile)

    def remote(src, dst, send_sem, recv_sem, to):
        return pltpu.make_async_remote_copy(
            src_ref=src,
            dst_ref=dst,
            send_sem=send_sem,
            recv_sem=recv_sem,
            device_id={"expert": to},
            device_id_type=MESH,
        )

    def plane_peer(k):
        return flipped(plane, k, planes)

    def place_peer(d):
        return flipped(place, d, experts)

    def each(first, last, step):
        lax.fori_loop(first, last, lambda i, carry: (step(i), carry)[1], 0)

    barrier = pltpu.get_barrier_semaphore()

    def greet_plane(k):
        to = plane_peer(k) * experts + place
        pl.semaphore_signal(barrier, inc=1, device_id={"expert": to}, device_id_type=MESH)

    def greet_place(d):
        to = plane * experts + place_peer(d)
        pl.semaphore_signal(barrier, inc=1, device_id={"expert": to}, device_id_type=MESH)

    each(1, planes, greet_plane)
    each(1, experts, greet_place)
    pl.semaphore_wait(barrier, planes + experts - 2)

    def route_copy(k, source):
        return remote(
            peer_routes.at[source],
            peer_routes.at[source],
            route_send_sem.at[k],
            route_recv_sem.at[source],
            plane_peer(k) * experts + place,
        )

    def token_copy(m, k, source):
        return remote(
            tokens.at[m, source],
            tokens.at[m, source],
            token_send_sem.at[m, k],
            token_recv_sem.at[m, source],
            plane_peer(k) * experts + place,
        )

    def out_copy(m, q, to, source):
        return remote(
            outbox.at[m, q, to],
            inbox.at[m, q, source],
            out_send_sem.at[m, q, to],
            in_recv_sem.at[m, q, source],
            plane * experts + to,
        )

    def out_local(m, q):
        return pltpu.make_async_copy(
            outbox.at[m, q, place], inbox.at[m, q, place], in_recv_sem.at[m, q, place]
        )

    def part_copy(m, q, to, source):
        return remote(
            partial.at[m, q, to],
            returned.at[m, q, source],
            part_send_sem.at[m, q, to],
            ret_recv_sem.at[m, q, source],
            plane * experts + to,
        )

    def part_local(m, q):
        return pltpu.make_async_copy(
            partial.at[m, q, place], returned.at[m, q, place], ret_recv_sem.at[m, q, place]
        )

    def back_copy(m, q, source):
        return remote(
            plane_send.at[m, q],
            plane_back.at[m, source],
            back_send_sem.at[m, q],
            back_recv_sem.at[m, source],
            q * experts + place,
        )

    def placing_of(r, m, q):
        chosen = peer_routes[q, pl.ds(r * micros + m, 1), :][:, :tok]
        onehot = lax.broadcasted_iota(jnp.int32, (experts, tok), 0) == chosen
        earlier = lax.broadcasted_iota(jnp.int32, (tok, tok), 0) < lax.broadcasted_iota(
            jnp.int32, (tok, tok), 1
        )
        counts = jnp.dot(
            onehot.astype(jnp.float32).astype(jnp.bfloat16),
            earlier.astype(jnp.float32).astype(jnp.bfloat16),
            preferred_element_type=jnp.float32,
        )
        slot = jnp.sum(jnp.where(onehot, counts, 0.0), axis=0, keepdims=True).astype(jnp.int32)
        flat = chosen * capacity + slot
        return (lax.broadcasted_iota(jnp.int32, (slots, tok), 0) == flat).astype(jnp.float32)

    def norm_and_send(r, m):
        source = acts_ref if r == 0 else out_ref
        if r > 0:
            each(1, planes, lambda k: token_copy(m, k, plane).wait_send())

        def add_squares(c, total):
            x = source[m, :, cols(c)].astype(jnp.float32)
            return total + jnp.sum(x * x, axis=1, keepdims=True)

        squares = lax.fori_loop(0, tiles, add_squares, jnp.zeros((tok, 1), jnp.float32))
        scale = lax.rsqrt(squares / width + 1e-06)

        def scaled(c):
            x = source[m, :, cols(c)].astype(jnp.float32)
            tokens[m, plane, :, cols(c)] = (x * scale * gain_ref[:, cols(c)]).astype(jnp.bfloat16)

        each(0, tiles, scaled)
        each(1, planes, lambda k: token_copy(m, k, plane).start())
        scores = jnp.dot(tokens[m, plane], router_ref[...], preferred_element_type=jnp.float32)
        chosen = route_cols_ref[r, m]
        onehot = lax.broadcasted_iota(jnp.int32, (tok, experts), 1) == chosen
        return jax.nn.sigmoid(jnp.sum(jnp.where(onehot, scores, 0.0), axis=1, keepdims=True))

    def pack(r, m, k):
        q = plane_peer(k)

        @pl.when(k > 0)
        def _():
            token_copy(m, k, q).wait_recv()

        if r > 0:
            each(1, experts, lambda d: out_copy(m, q, place_peer(d), place).wait_send())
        placing = placing_of(r, m, q).astype(jnp.bfloat16)

        def packed(c):
            rows = jnp.dot(placing, tokens[m, q, :, cols(c)], preferred_element_type=jnp.float32)
            outbox[m, q, :, :, cols(c)] = rows.astype(jnp.bfloat16).reshape(
                experts, capacity, tile
            )

        each(0, tiles, packed)
        out_local(m, q).start()
        each(1, experts, lambda d: out_copy(m, q, place_peer(d), place).start())

    def expert(r, m, k):
        q = plane_peer(k)
        out_local(m, q).wait()

        def arrived(d):
            out_copy(m, q, place_peer(d), place_peer(d)).wait_recv()

        each(1, experts, arrived)
        if r > 0:
            each(1, experts, lambda d: part_copy(m, q, place_peer(d), place).wait_send())
        rows = inbox[m, q].reshape(slots, width)
        gate_proj = jnp.dot(rows, gate_ref[...], preferred_element_type=jnp.float32)
        up_proj = jnp.dot(rows, up_ref[...], preferred_element_type=jnp.float32)
        hidden = (jax.nn.silu(gate_proj) * up_proj).astype(jnp.bfloat16)

        def projected(c):
            part = jnp.dot(hidden, down_ref[:, cols(c)], preferred_element_type=jnp.float32)
            partial[m, q, :, :, cols(c)] = part.astype(jnp.bfloat16).reshape(
                experts, capacity, tile
            )

        each(0, tiles, projected)
        part_local(m, q).start()
        each(1, experts, lambda d: part_copy(m, q, place_peer(d), place).start())

    def unpack(r, m, k):
        q = plane_peer(k)
        part_local(m, q).wait()

        def arrived(d):
            part_copy(m, q, place_peer(d), place_peer(d)).wait_recv()

        each(1, experts, arrived)
        if r > 0:

            @pl.when(k > 0)
            def _():
                back_copy(m, q, plane).wait_send()

        picking = placing_of(r, m, q).T.astype(jnp.bfloat16)

        def picked(c):
            rows = returned[m, q, :, :, cols(c)].reshape(slots, tile)
            plane_send[m, q, :, cols(c)] = jnp.dot(
                picking, rows, preferred_element_type=jnp.float32
            ).astype(jnp.bfloat16)

        each(0, tiles, picked)

        @pl.when(k > 0)
        def _():
            back_copy(m, q, plane).start()

    def finish(r, m, gate_val):
        source = acts_ref if r == 0 else out_ref
        each(1, planes, lambda k: back_copy(m, plane_peer(k), plane_peer(k)).wait_recv())

        def summed(c):
            total = plane_send[m, plane, :, cols(c)].astype(jnp.float32)
            for k in range(1, planes):
                total += plane_back[m, plane_peer(k), :, cols(c)].astype(jnp.float32)
            x = source[m, :, cols(c)].astype(jnp.float32)
            out_ref[m, :, cols(c)] = (x + gate_val * total).astype(jnp.bfloat16)

        each(0, tiles, summed)

    def steps(phase, r, m):
        each(0, planes, lambda k: phase(r, m, k))

    peer_routes[plane] = route_rows_ref[...]
    each(1, planes, lambda k: route_copy(k, plane).start())
    gates = {}
    gates[0] = norm_and_send(0, 0)
    each(1, planes, lambda k: route_copy(k, plane_peer(k)).wait_recv())
    steps(pack, 0, 0)
    for r in range(rounds):
        for m in range(micros):
            after = m + 1 if m + 1 < micros else 0
            after_round = r if m + 1 < micros else r + 1
            if m + 1 < micros:
                if r == 0:
                    gates[after] = norm_and_send(r, after)
                steps(expert, r, m)
                steps(pack, r, after)
            else:
                ahead = after_round < rounds and micros > 1
                if ahead:
                    steps(unpack, r, 0)
                    finish(r, 0, gates[0])
                    gates[0] = norm_and_send(r + 1, 0)
                steps(expert, r, m)
                if ahead:
                    steps(pack, r + 1, 0)
                for other in range(1 if ahead else 0, micros):
                    steps(unpack, r, other)
                    finish(r, other, gates[other])
                    if r + 1 < rounds and other > 0:
                        gates[other] = norm_and_send(r + 1, other)
                if r + 1 < rounds and micros == 1:
                    gates[0] = norm_and_send(r + 1, 0)
                    steps(pack, r + 1, 0)

    each(1, planes, lambda k: route_copy(k, plane).wait_send())
    for m in range(micros):
        each(1, planes, lambda k: token_copy(m, k, plane).wait_send())

        def sent(k):
            q = plane_peer(k)
            each(1, experts, lambda d: out_copy(m, q, place_peer(d), place).wait_send())
            each(1, experts, lambda d: part_copy(m, q, place_peer(d), place).wait_send())

            @pl.when(k > 0)
            def _():
                back_copy(m, q, plane).wait_send()

        each(0, planes, sent)


def run_layers(acts, gain, router, routes, gate_mat, up_mat, down_mat):
    devices = lax.axis_size("expert")
    experts = router.shape[1]
    planes = devices // experts
    micros, tok, width = acts.shape
    rounds = routes.shape[0]
    capacity = 2 * tok // experts
    hidden = gate_mat.shape[1]
    rows = rounds * micros
    row_pad, lane_pad = -(-rows // 8) * 8, -(-tok // 128) * 128
    route_rows = jnp.pad(
        routes.reshape(rows, tok), ((0, row_pad - rows), (0, lane_pad - tok))
    )
    vmem = pl.BlockSpec(memory_space=pltpu.VMEM)
    dma = pltpu.SemaphoreType.DMA
    slot_shape = (micros, planes, experts, capacity, width)
    plane_shape = (micros, planes, tok, width)
    slots = experts * capacity
    flops = 2 * rows * planes * slots * width * hidden * 3
    return pl.pallas_call(
        functools.partial(layers_kernel, rounds, micros, planes, experts, capacity),
        out_shape=jax.ShapeDtypeStruct(acts.shape, acts.dtype),
        in_specs=[vmem] * 8,
        out_specs=vmem,
        scratch_shapes=[
            pltpu.VMEM((planes, row_pad, lane_pad), jnp.int32),
            pltpu.VMEM(plane_shape, jnp.bfloat16),
            pltpu.VMEM(slot_shape, jnp.bfloat16),
            pltpu.VMEM(slot_shape, jnp.bfloat16),
            pltpu.VMEM(slot_shape, jnp.bfloat16),
            pltpu.VMEM(slot_shape, jnp.bfloat16),
            pltpu.VMEM(plane_shape, jnp.bfloat16),
            pltpu.VMEM(plane_shape, jnp.bfloat16),
            dma((planes,)),
            dma((planes,)),
            dma((micros, planes)),
            dma((micros, planes)),
            dma((micros, planes, experts)),
            dma((micros, planes, experts)),
            dma((micros, planes, experts)),
            dma((micros, planes, experts)),
            dma((micros, planes)),
            dma((micros, planes)),
        ],
        compiler_params=pltpu.CompilerParams(
            collective_id=0, has_side_effects=True, vmem_limit_bytes=62 * 1024 * 1024
        ),
        cost_estimate=pl.CostEstimate(
            flops=flops,
            bytes_accessed=3 * gate_mat.size * 2 + 4 * acts.size,
            transcendentals=rows * planes * slots * hidden,
        ),
    )(acts, gain, router, route_rows, routes, gate_mat, up_mat, down_mat)


def body(acts, norm_gain, router, routes, w_gate, w_up, w_down):
    sections = lax.axis_size("section")
    rounds = routes.shape[1]
    weights = (w_gate[0, 0], w_up[0, 0], w_down[0, 0])
    if sections == 1:
        return run_layers(acts[0], norm_gain, router[0], routes[0], *weights)[None]
    carried = acts[0]
    pairs = [(source, (source + 1) % sections) for source in range(sections)]
    for r in range(rounds):
        carried = run_layers(carried, norm_gain, router[0], routes[0, r : r + 1], *weights)
        carried = lax.ppermute(carried, "section", pairs)
    return carried[None]


def solution(mesh):
    in_specs = (
        P("section", None, "expert", None),
        P("section", None),
        P("section", None, None),
        P("section", None, None, "expert", None),
        P("section", "expert", None, None),
        P("section", "expert", None, None),
        P("section", "expert", None, None),
    )
    out_specs = P("section", None, "expert", None)
    return jax.shard_map(body, mesh=mesh, in_specs=in_specs, out_specs=out_specs, check_vma=False)
```

time: 740 us -> 417 us (0.56)
  waiting for transfers between devices: 571 us -> 0 us
  Pallas kernels: 0 us -> 410 us
  matrix products: 58 us -> 0 us
  starting transfers between devices: 53.1 us -> 0 us
  other arithmetic: 25.7 us -> 0 us
  local copies, waits for them, and re-layouts: 27.5 us -> 6.94 us
    all_to_all x8 -> x0, waiting for transfers between devices: 571 us -> none  [the longest x4 291 us: apply_layer(): lax.all_to_all(sendout, 'expert', split_axis=0, concat_axis=0, tiled=True)]
    pallas_call x0 -> x1, Pallas kernels: none -> 410 us  [run_layers(): pl.pallas_call(functools.partial(layers_kernel, rounds, micros, planes, e...]
    dot_general x16 -> x0, matrix products: 58 us -> none  [the longest x4 34 us: expert_compute(): jnp.dot(hidden, down_mat, preferred_element_type=jnp.float32)]
    all_to_all x8 -> x0, starting transfers between devices: 53 us -> none  [the longest x4 26.6 us: expert_work(): lax.all_to_all(expert_compute(rows_box), 'expert', split_axis=0, concat_a...]
    reduce_sum x9 -> x0, other arithmetic: 18.1 us -> none  [the longest x4 16.1 us: apply_layer(): jnp.sum(returned.reshape(group_size, experts_here, capacity, width).astyp...]
    gather x4 -> x0, local copies, waits for them, and re-layouts: 14.7 us -> none  [apply_layer(): picked = jnp.take(combined, flat_slot, axis=0)]
    broadcast_in_dim x4 -> x0, local copies, waits for them, and re-layouts: 11.5 us -> none  [apply_layer(): jnp.broadcast_to(outbox[None], (group_size, experts_here, capacity, width))]
  transfers between devices with their start and end apart: 12 -> 0, of which waited for: 8 -> 0; matrix products, arithmetic and copies ran while one was open for 11% -> 0% of each run, Pallas kernels for 0% -> 0%
where the time goes in v1:
time: 417 us
  Pallas kernels  410 us (98%)
  local copies, waits for them, and re-layouts  6.94 us (2%)
    pallas_call x1, Pallas kernels, run_layers(): pl.pallas_call(functools.partial(layers_kernel, rounds, micros, planes, e...  410 us

profile of v1, /device:TPU:11, one launch (start us, length us, event | category | flops | bytes accessed | tf_op | source)
XLA Modules:
  0.0 416.9 jit_solution(13997655400151163488)
XLA Ops:
  0.0 1.3 pad.4.route_rows_ref
  1.3 1.5 copy.10.route_cols_ref
  2.7 2.1 copy.9
  4.8 410.0 %shard_map.73 = bf16[2,64,3584]{2,1,0:T(8,128)(2,1)} custom-call(bf16[2,64,3584]{2,1,0:T(8,128)(2,1)} %bitcast.15, f32[1,3584]{1,0:T(1,128)} %gain_ref.1, bf16[3584,8]{1,0:T(8,128)(2,1)} %bitcast.9, s32[8,128]{1,0:T(8,128)} %pad.4.route_rows_ref, s32[2,2,64,1]{3,2,1,0:T(8,128)} %copy.10.route_cols_ref, bf16[3584,256]{1,0:T(8,128)(2,1)} %bitcast.12, ...), custom_call_target="tpu_custom_call" | custom-call | flops 11274289152 | bytes 7340032 | tf_op jit(solution)/shard_map/pallas_call | solution.py:356
  414.8 2.2 copy.12

commit v2 on v1

--- a/solution.py
+++ b/solution.py
@@ -18,11 +18,73 @@
     return total
 
 
+def at_least(a, b):
+    return (a - b + (1 << 16)) // (1 << 16)
+
+
+def nearest(plane, j, planes):
+    above_is_more = at_least(planes - 1 - plane, plane + 1)
+    paired = above_is_more * plane + (1 - above_is_more) * (planes - 1 - plane)
+    in_pairs = at_least(2 * paired, j)
+    of_pair = (j + 1) // 2 * (1 - 2 * (j % 2))
+    beyond = (j - paired) * (2 * above_is_more - 1)
+    return plane + in_pairs * of_pair + (1 - in_pairs) * beyond
+
+
 def column_tile(width):
     for tile in (512, 256, 128):
         if width % tile == 0:
             return tile
     return width
+
+
+def order_of_work(rounds, micros, planes):
+    work = [(r, m) for r in range(rounds) for m in range(micros)]
+    stages = {}
+    for r, m in work:
+        stages[r, m] = {
+            kind: [(kind, r, m, k) for k in range(planes)] for kind in ("pack", "expert", "unpack")
+        }
+    order = [("norm", 0, 0, 0), ("routes", 0, 0, 0)]
+    left = []
+    for at, (r, m) in enumerate(work):
+        mine = stages[r, m]
+        packs, experts = mine["pack"], mine["expert"]
+        if at == 0:
+            order += packs[:2]
+            for k in range(2, planes):
+                order += [experts[k - 2], packs[k]]
+            done = planes - 2
+        else:
+            rest = packs[1:]
+            while rest or left:
+                order += rest[:1]
+                rest = rest[1:]
+                order += left[:1]
+                left = left[1:]
+                if not rest and len(left) == 2:
+                    break
+            done = 0
+            before = work[at - 1]
+            while left:
+                order += [experts[done], left[0]]
+                left = left[1:]
+                done += 1
+            order += [experts[done]]
+            done += 1
+            order += [("finish", before[0], before[1], 0)]
+        if at + 1 < len(work):
+            nxt = work[at + 1]
+            if micros == 1:
+                order += experts[done:] + mine["unpack"] + [("finish", r, m, 0)]
+                order += [("norm", nxt[0], nxt[1], 0), stages[nxt]["pack"][0]]
+                left, done = [], planes
+            else:
+                order += [("norm", nxt[0], nxt[1], 0), stages[nxt]["pack"][0]]
+                left = experts[done:] + mine["unpack"]
+        else:
+            order += experts[done:] + mine["unpack"] + [("finish", r, m, 0)]
+    return order
 
 
 def layers_kernel(
@@ -111,14 +173,26 @@
             plane_peer(k) * experts + place,
         )
 
-    def token_copy(m, k, source):
+    def token_copy(m, source, step):
+        slot = source if step == 1 else source + at_least(source, plane) * at_least(plane, source) * (
+            planes - source
+        )
         return remote(
             tokens.at[m, source],
             tokens.at[m, source],
-            token_send_sem.at[m, k],
+            token_send_sem.at[m, slot],
             token_recv_sem.at[m, source],
-            plane_peer(k) * experts + place,
-        )
+            (me + (step + planes) * experts) % (planes * experts),
+        )
+
+    def passing(m, q, act):
+        @pl.when(jnp.logical_and(q <= plane, plane < planes - 1))
+        def _():
+            act(token_copy(m, q, 1))
+
+        @pl.when(jnp.logical_and(q >= plane, plane > 0))
+        def _():
+            act(token_copy(m, q, -1))
 
     def out_copy(m, q, to, source):
         return remote(
@@ -175,7 +249,7 @@
     def norm_and_send(r, m):
         source = acts_ref if r == 0 else out_ref
         if r > 0:
-            each(1, planes, lambda k: token_copy(m, k, plane).wait_send())
+            passing(m, plane, lambda copy: copy.wait_send())
 
         def add_squares(c, total):
             x = source[m, :, cols(c)].astype(jnp.float32)
@@ -189,18 +263,17 @@
             tokens[m, plane, :, cols(c)] = (x * scale * gain_ref[:, cols(c)]).astype(jnp.bfloat16)
 
         each(0, tiles, scaled)
-        each(1, planes, lambda k: token_copy(m, k, plane).start())
+        passing(m, plane, lambda copy: copy.start())
         scores = jnp.dot(tokens[m, plane], router_ref[...], preferred_element_type=jnp.float32)
         chosen = route_cols_ref[r, m]
         onehot = lax.broadcasted_iota(jnp.int32, (tok, experts), 1) == chosen
         return jax.nn.sigmoid(jnp.sum(jnp.where(onehot, scores, 0.0), axis=1, keepdims=True))
 
     def pack(r, m, k):
-        q = plane_peer(k)
-
-        @pl.when(k > 0)
-        def _():
-            token_copy(m, k, q).wait_recv()
+        q = nearest(plane, k, planes)
+        if k > 0:
+            token_copy(m, q, 1).wait_recv()
+            passing(m, q, lambda copy: copy.start())
 
         if r > 0:
             each(1, experts, lambda d: out_copy(m, q, place_peer(d), place).wait_send())
@@ -217,7 +290,7 @@
         each(1, experts, lambda d: out_copy(m, q, place_peer(d), place).start())
 
     def expert(r, m, k):
-        q = plane_peer(k)
+        q = nearest(plane, k, planes)
         out_local(m, q).wait()
 
         def arrived(d):
@@ -242,17 +315,16 @@
         each(1, experts, lambda d: part_copy(m, q, place_peer(d), place).start())
 
     def unpack(r, m, k):
-        q = plane_peer(k)
+        q = nearest(plane, k, planes)
         part_local(m, q).wait()
 
         def arrived(d):
             part_copy(m, q, place_peer(d), place_peer(d)).wait_recv()
 
         each(1, experts, arrived)
-        if r > 0:
-
-            @pl.when(k > 0)
-            def _():
+        if k > 0:
+            passing(m, q, lambda copy: copy.wait_send())
+            if r > 0:
                 back_copy(m, q, plane).wait_send()
 
         picking = placing_of(r, m, q).T.astype(jnp.bfloat16)
@@ -265,8 +337,7 @@
 
         each(0, tiles, picked)
 
-        @pl.when(k > 0)
-        def _():
+        if k > 0:
             back_copy(m, q, plane).start()
 
     def finish(r, m, gate_val):
@@ -282,45 +353,26 @@
 
         each(0, tiles, summed)
 
-    def steps(phase, r, m):
-        each(0, planes, lambda k: phase(r, m, k))
-
     peer_routes[plane] = route_rows_ref[...]
     each(1, planes, lambda k: route_copy(k, plane).start())
     gates = {}
-    gates[0] = norm_and_send(0, 0)
-    each(1, planes, lambda k: route_copy(k, plane_peer(k)).wait_recv())
-    steps(pack, 0, 0)
-    for r in range(rounds):
-        for m in range(micros):
-            after = m + 1 if m + 1 < micros else 0
-            after_round = r if m + 1 < micros else r + 1
-            if m + 1 < micros:
-                if r == 0:
-                    gates[after] = norm_and_send(r, after)
-                steps(expert, r, m)
-                steps(pack, r, after)
-            else:
-                ahead = after_round < rounds and micros > 1
-                if ahead:
-                    steps(unpack, r, 0)
-                    finish(r, 0, gates[0])
-                    gates[0] = norm_and_send(r + 1, 0)
-                steps(expert, r, m)
-                if ahead:
-                    steps(pack, r + 1, 0)
-                for other in range(1 if ahead else 0, micros):
-                    steps(unpack, r, other)
-                    finish(r, other, gates[other])
-                    if r + 1 < rounds and other > 0:
-                        gates[other] = norm_and_send(r + 1, other)
-                if r + 1 < rounds and micros == 1:
-                    gates[0] = norm_and_send(r + 1, 0)
-                    steps(pack, r + 1, 0)
+    for kind, r, m, k in order_of_work(rounds, micros, planes):
+        if kind == "norm":
+            gates[m] = norm_and_send(r, m)
+        elif kind == "routes":
+            each(1, planes, lambda k: route_copy(k, plane_peer(k)).wait_recv())
+        elif kind == "pack":
+            pack(r, m, k)
+        elif kind == "expert":
+            expert(r, m, k)
+        elif kind == "unpack":
+            unpack(r, m, k)
+        else:
+            finish(r, m, gates[m])
 
     each(1, planes, lambda k: route_copy(k, plane).wait_send())
     for m in range(micros):
-        each(1, planes, lambda k: token_copy(m, k, plane).wait_send())
+        passing(m, plane, lambda copy: copy.wait_send())
 
         def sent(k):
             q = plane_peer(k)
@@ -369,7 +421,7 @@
             pltpu.VMEM(plane_shape, jnp.bfloat16),
             dma((planes,)),
             dma((planes,)),
-            dma((micros, planes)),
+            dma((micros, planes + 1)),
             dma((micros, planes)),
             dma((micros, planes, experts)),
             dma((micros, planes, experts)),

time: 417 us -> 375 us (0.90); the launches traced: 417 us -> 370 us
  Pallas kernels: 410 us -> 363 us
    pallas_call x1, Pallas kernels: 410 us -> 363 us  [run_layers(): pl.pallas_call(functools.partial(layers_kernel, rounds, micros, planes, e...]
where the time goes in v2:
time: 375 us; the launch traced here: 370 us
  Pallas kernels  363 us (97%)
  local copies, waits for them, and re-layouts  6.94 us (2%)
    pallas_call x1, Pallas kernels, run_layers(): pl.pallas_call(functools.partial(layers_kernel, rounds, micros, planes, e...  363 us

profile of v2, /device:TPU:11, one launch (start us, length us, event | category | flops | bytes accessed | tf_op | source)
XLA Modules:
  0.0 369.9 jit_solution(15231735933110269026)
XLA Ops:
  0.0 1.3 pad.4.route_rows_ref
  1.3 1.5 copy.10.route_cols_ref
  2.7 2.1 copy.9
  4.8 363.0 %shard_map.73 = bf16[2,64,3584]{2,1,0:T(8,128)(2,1)} custom-call(bf16[2,64,3584]{2,1,0:T(8,128)(2,1)} %bitcast.15, f32[1,3584]{1,0:T(1,128)} %gain_ref.1, bf16[3584,8]{1,0:T(8,128)(2,1)} %bitcast.9, s32[8,128]{1,0:T(8,128)} %pad.4.route_rows_ref, s32[2,2,64,1]{3,2,1,0:T(8,128)} %copy.10.route_cols_ref, bf16[3584,256]{1,0:T(8,128)(2,1)} %bitcast.12, ...), custom_call_target="tpu_custom_call" | custom-call | flops 11274289152 | bytes 7340032 | tf_op jit(solution)/shard_map/pallas_call | solution.py:408
  367.8 2.2 copy.12
